TPU v7x, 32 devices: a whole 2x2x4 slice. The times are simulated.
32 devices in a mesh: req: 8 (over y, x, core), tp: 4 (over z).
Axes of the slice: x: 2, y: 2, z: 4, core: 2. Of those that a mesh axis runs over, the one named last changes fastest.
Arguments:
- activations: bfloat16 [2048, 2304], P('req'), may hold values from -6 to 6
- lengths: int32 [8, 4], P('req'), may hold values from 1 to 192, 256 in all within a row
- adapter_of: int32 [8, 4], P('req'), may hold values from 0 to 15
- slot_of: int32 [16], replicated, may hold values from 0 to 15, as said below
- page_table: int32 [8, 6], P('req'), may hold values from 0 to 5, each once within a row
- experts_of: int32 [2048, 2], P('req'), may hold values from 0 to 7, all different within a row; in each aligned block of 256 rows (0 to 255, 256 to 511, ...) at most 72 rows name the same one
- attn_gain: float32 [2304], replicated, may hold values from 0.25 to 1.75
- moe_gain: float32 [2304], replicated, may hold values from 0.25 to 1.75
- w_qkv: bfloat16 [2304, 3, 2304], P(None, None, 'tp'), may hold values from -4 to 4
- output_weight: bfloat16 [2304, 2304], P('tp'), may hold values from -0.125 to 0.125
- router: bfloat16 [2304, 8], replicated, may hold values from -0.125 to 0.125
- w_gate_up: bfloat16 [8, 2304, 2, 5760], P('req', None, None, 'tp'), may hold values from -0.125 to 0.125
- w_down: bfloat16 [8, 5760, 2304], P('req', 'tp'), may hold values from -0.078125 to 0.078125
- expert_up_factors: bfloat16 [8, 256, 2, 5760], P('req', None, None, 'tp'), may hold values from -0.59765625 to 0.59765625
- pool_a: bfloat16 [16, 2304, 64], P('req'), may hold values from -0.125 to 0.125
- slot_query_key_value_up: bfloat16 [16, 16, 3, 2304], P('req', None, None, 'tp'), may hold values from -0.59765625 to 0.59765625
- pool_aout: bfloat16 [16, 2304, 16], P('req', 'tp'), may hold values from -0.125 to 0.125
- pool_bout: bfloat16 [16, 16, 2304], P('req'), may hold values from -1.796875 to 1.796875
Outputs:
- layer_out: bfloat16 [2048, 2304], P('req')
- page_cache: bfloat16 [48, 128, 2, 2304], P('req', None, None, 'tp')
Inputs may be any that keep to these rules, and one draw needn't show every extreme that they name: `slot_of`: distinct slots. `page_table`: each row holds every page index once. `experts_of`: the two experts of a token differ; among the 256 tokens of one index of req at most 72 choose one expert, and some expert reaches 72.
All inputs are finite; a program needn't handle non-finite values.
Results may differ from a plain program's by a relative error of at most 0.0095.
Values may be sent and summed in bfloat16 or wider, within the bound.
A program may use at most 128 MiB of HBM per device.

v0:
```python
import math
import jax
import jax.numpy as jnp
from jax import lax
from jax.sharding import PartitionSpec as P

D = 2304
HEAD_SIZE = 64
EXPERTS = 8
ADAPTER_RANK = 16
ADAPTER_TOTAL = 16
PAGE = 128
CAP = 72
epsilon = 1e-05
adapter_scale = 2.0
rope_base = 10000.0


def rms_norm(values, scales):
    mean_sq = jnp.mean(values * values, axis=-1, keepdims=True)
    return values * lax.rsqrt(mean_sq + epsilon) * scales


def token_layout(lengths_row, tok_count):
    ends_at = jnp.cumsum(lengths_row)
    starts = ends_at - lengths_row
    places = jnp.arange(tok_count, dtype=jnp.int32)
    request = jnp.sum((places[:, None] >= ends_at[None, :]).astype(jnp.int32), axis=1)
    position = places - starts[request]
    return (request, position)


def rotate(values, position):
    head_dim = values.shape[-1]
    half_dim = head_dim // 2
    frequency = rope_base ** (-jnp.arange(half_dim, dtype=jnp.float32) * 2.0 / head_dim)
    angles = position.astype(jnp.float32)[:, None] * frequency[None, :]
    cosine = jnp.cos(angles)[:, None, :]
    sine_part = jnp.sin(angles)[:, None, :]
    front_half = values[..., :half_dim]
    back_half = values[..., half_dim:]
    return jnp.concatenate(
        [front_half * cosine - back_half * sine_part, back_half * cosine + front_half * sine_part],
        axis=-1,
    )


def per_device(
    activations,
    lengths,
    adapter_of,
    slot_of,
    page_table,
    experts_of,
    attn_gain,
    moe_gain,
    w_qkv,
    output_weight,
    router,
    w_gate_up,
    w_down,
    expert_up_factors,
    pool_a,
    slot_query_key_value_up,
    pool_aout,
    pool_bout,
):
    token_share = activations.shape[0]
    n_req = lax.axis_size("req")
    request, position = token_layout(lengths[0], token_share)
    adapter = adapter_of[0][request]
    token_slot = slot_of[adapter]
    pool_down, slot_up_factors, pool_head, pool_outup = (
        lax.all_gather(pool_a, "req", axis=0, tiled=True),
        lax.all_gather(slot_query_key_value_up, "req", axis=0, tiled=True),
        lax.all_gather(pool_aout, "req", axis=0, tiled=True),
        lax.all_gather(pool_bout, "req", axis=0, tiled=True),
    )
    slot_count = pool_down.shape[0]
    slot_hot = token_slot[:, None] == jnp.arange(slot_count, dtype=jnp.int32)[None, :]
    head_width = w_qkv.shape[2]
    heads_number = head_width // HEAD_SIZE
    normed = rms_norm(activations.astype(jnp.float32), attn_gain).astype(jnp.bfloat16)
    down_all = jnp.einsum(
        "td,sdr->tsr",
        normed,
        pool_down[:, :, : 3 * ADAPTER_RANK],
        preferred_element_type=jnp.float32,
    )
    coeff_qkv = jnp.sum(jnp.where(slot_hot[:, :, None], down_all, 0.0), axis=1).astype(jnp.bfloat16)
    spread_rows = jnp.where(
        slot_hot[:, :, None, None],
        coeff_qkv.reshape(token_share, 1, 3, ADAPTER_RANK),
        jnp.zeros((), jnp.bfloat16),
    )
    adapter_query_key_value = jnp.einsum(
        "qwxv,wvxd->qxd", spread_rows, slot_up_factors, preferred_element_type=jnp.float32
    )
    plain_query_key_value = jnp.dot(
        normed, w_qkv.reshape(D, 3 * head_width), preferred_element_type=jnp.float32
    ).reshape(token_share, 3, head_width)
    projection_result = (plain_query_key_value + adapter_scale * adapter_query_key_value).reshape(
        token_share, 3, heads_number, HEAD_SIZE
    )
    queries = rotate(projection_result[:, 0], position).astype(jnp.bfloat16)
    keys_roped = rotate(projection_result[:, 1], position).astype(jnp.bfloat16)
    values = projection_result[:, 2].astype(jnp.bfloat16)
    pool_dev = page_table.shape[1]
    pages_used = (lengths[0] + PAGE - 1) // PAGE
    first_page = jnp.cumsum(pages_used) - pages_used
    local_page = page_table[0][first_page[request] + position // PAGE]
    cache_row = local_page * PAGE + position % PAGE
    place_hot = (
        jnp.arange(pool_dev * PAGE, dtype=jnp.int32)[:, None] == cache_row[None, :]
    ).astype(jnp.bfloat16)
    key_value = jnp.stack(
        [keys_roped.reshape(token_share, head_width), values.reshape(token_share, head_width)],
        axis=1,
    ).reshape(token_share, 2 * head_width)
    page_cache = (
        jnp.dot(place_hot, key_value, preferred_element_type=jnp.float32)
        .astype(jnp.bfloat16)
        .reshape(pool_dev, PAGE, 2, head_width)
    )
    scores = jnp.einsum("qhd,khd->hqk", queries, keys_roped, preferred_element_type=jnp.float32) * (
        1.0 / math.sqrt(HEAD_SIZE)
    )
    allowed = (request[:, None] == request[None, :]) & (position[None, :] <= position[:, None])
    scores = jnp.where(allowed[None], scores, -1e30)
    row_max = jnp.max(scores, axis=-1, keepdims=True)
    weights = jnp.exp(scores - row_max)
    weights = (weights / jnp.sum(weights, axis=-1, keepdims=True)).astype(jnp.bfloat16)
    attention_result = (
        jnp.einsum("hqk,khd->qhd", weights, values, preferred_element_type=jnp.float32)
        .astype(jnp.bfloat16)
        .reshape(token_share, head_width)
    )
    aout_all = jnp.einsum(
        "tc,scr->tsr", attention_result, pool_head, preferred_element_type=jnp.float32
    )
    coeff_out = jnp.sum(jnp.where(slot_hot[:, :, None], aout_all, 0.0), axis=1)
    spread_out = jnp.where(slot_hot[:, :, None], coeff_out[:, None, :], 0.0).reshape(
        token_share, slot_count * ADAPTER_RANK
    )
    output_update = jnp.dot(
        spread_out,
        pool_outup.astype(jnp.float32).reshape(slot_count * ADAPTER_RANK, D),
        precision=lax.Precision.HIGHEST,
    )
    head_term = (
        jnp.dot(attention_result, output_weight, preferred_element_type=jnp.float32)
        + adapter_scale * output_update
    )
    mixed_out = lax.psum(head_term, "tp")
    residual_stream = activations.astype(jnp.float32) + mixed_out
    normed_moe = rms_norm(residual_stream, moe_gain).astype(jnp.bfloat16)
    logits = jnp.dot(normed_moe, router, preferred_element_type=jnp.float32)
    chosen = jnp.take_along_axis(logits, experts_of, axis=1)
    gate_weights = 1.0 / (1.0 + jnp.exp(chosen[:, ::-1] - chosen))
    exp_all = jnp.einsum(
        "td,sdr->tsr",
        normed_moe,
        pool_down[:, :, 3 * ADAPTER_RANK :],
        preferred_element_type=jnp.float32,
    )
    coeff_exp = jnp.sum(jnp.where(slot_hot[:, :, None], exp_all, 0.0), axis=1).astype(jnp.bfloat16)
    capacity = CAP
    split_count = n_req // EXPERTS
    flat_expert = experts_of.reshape(-1)
    expert_hot = (flat_expert[:, None] == jnp.arange(EXPERTS, dtype=jnp.int32)[None, :]).astype(
        jnp.int32
    )
    order_in = jnp.sum((jnp.cumsum(expert_hot, axis=0) - expert_hot) * expert_hot, axis=1)
    column = flat_expert * capacity + order_in
    pick = (column[:, None] == jnp.arange(EXPERTS * capacity, dtype=jnp.int32)[None, :]).reshape(
        token_share, 2, EXPERTS * capacity
    )
    route = jnp.any(pick, axis=1).astype(jnp.bfloat16)
    combine_weights = jnp.sum(jnp.where(pick, gate_weights[:, :, None], 0.0), axis=1)

    def spread_copies(array):
        shaped = array.reshape((EXPERTS, 1, capacity) + array.shape[1:])
        return jnp.broadcast_to(shaped, (EXPERTS, split_count, capacity) + array.shape[1:]).reshape(
            (n_req, capacity) + array.shape[1:]
        )

    send_coeff = jnp.einsum(
        "ts,tr->sr", route, coeff_exp, preferred_element_type=jnp.float32
    ).astype(jnp.bfloat16)
    send_ids = jnp.einsum(
        "ts,t->s", route, adapter.astype(jnp.bfloat16), preferred_element_type=jnp.float32
    ).astype(jnp.bfloat16)
    adapter_range = jnp.arange(ADAPTER_TOTAL, dtype=jnp.int32).astype(jnp.bfloat16)
    send_rows = jnp.einsum(
        "ts,td->sd", route, normed_moe, preferred_element_type=jnp.float32
    ).astype(jnp.bfloat16)
    expert_input_rows = lax.all_to_all(
        spread_copies(send_rows), "req", split_axis=0, concat_axis=0, tiled=True
    )
    coeff_rank = lax.all_to_all(
        spread_copies(send_coeff), "req", split_axis=0, concat_axis=0, tiled=True
    )
    adapter_ids = lax.all_to_all(
        spread_copies(send_ids), "req", split_axis=0, concat_axis=0, tiled=True
    )
    count = expert_input_rows.shape[1]
    flat_rows = expert_input_rows.reshape(n_req * count, D)
    flat_coeff = coeff_rank.reshape(n_req * count, ADAPTER_RANK)
    flat_ids = adapter_ids.reshape(n_req * count)
    unit_count = w_gate_up.shape[3]
    broad_coefficients = jnp.where(
        flat_ids[:, None, None] == adapter_range[None, :, None],
        flat_coeff[:, None, :],
        jnp.zeros((), jnp.bfloat16),
    ).reshape(n_req * count, ADAPTER_TOTAL * ADAPTER_RANK)
    before_norm = jnp.dot(
        flat_rows, w_gate_up[0].reshape(D, 2 * unit_count), preferred_element_type=jnp.float32
    )
    before_norm = before_norm + adapter_scale * jnp.dot(
        broad_coefficients,
        expert_up_factors[0].reshape(ADAPTER_TOTAL * ADAPTER_RANK, 2 * unit_count),
        preferred_element_type=jnp.float32,
    )
    hidden = (jax.nn.silu(before_norm[:, :unit_count]) * before_norm[:, unit_count:]).astype(
        jnp.bfloat16
    )
    partial_term = jnp.dot(hidden, w_down[0], preferred_element_type=jnp.float32).astype(
        jnp.bfloat16
    )
    returned = lax.all_to_all(
        partial_term.reshape(n_req, count, D), "req", split_axis=0, concat_axis=0, tiled=True
    )
    summed = jnp.sum(
        returned.astype(jnp.float32).reshape(EXPERTS, split_count, capacity, D), axis=1
    ).reshape(EXPERTS * capacity, D)
    moe_part = jnp.dot(combine_weights, summed, precision=lax.Precision.HIGHEST)
    moe_sum = lax.psum(moe_part.astype(jnp.bfloat16), "tp").astype(jnp.float32)
    layer_out = (residual_stream + moe_sum).astype(jnp.bfloat16)
    return (layer_out, page_cache)


def solution(mesh):
    return jax.shard_map(
        per_device,
        mesh=mesh,
        in_specs=(
            P("req", None),
            P("req", None),
            P("req", None),
            P(),
            P("req", None),
            P("req", None),
            P(),
            P(),
            P(None, None, "tp"),
            P("tp", None),
            P(),
            P("req", None, None, "tp"),
            P("req", "tp", None),
            P("req", None, None, "tp"),
            P("req", None, None),
            P("req", None, None, "tp"),
            P("req", "tp", None),
            P("req", None, None),
        ),
        out_specs=(P("req", None), P("req", None, None, "tp")),
        check_vma=False,
    )
```

profile of v0, /device:TPU:0, one launch (start us, length us, event | category | flops | bytes accessed | tf_op | source)
XLA Modules:
  0.0 364.0 jit_solution(4491412793175182737)
XLA Ops:
  7.2 0.7 all-gather.3.cloned.1.call-update
  8.0 0.7 all-gather.5.cloned.1.call-update
  9.4 0.8 reduce-window.27
  10.4 0.8 bitcast_subtract_fusion.2
  11.3 1.6 fusion.10
  12.9 1.5 fusion.63
  14.3 1.5 fusion.66
  15.8 2.0 fusion.62
  17.8 6.8 %compare_select_fusion.9 = (s32[256,1]{0,1:T(1,128)S(1)}, s32[256,1]{0,1:T(1,128)S(1)}, s32[256,1]{0,1:T(1,128)S(1)}) fusion(s32[]{:T(128)} %bitcast.20, s32[]{:T(128)} %bitcast.21, s32[]{:T(128)} %bitcast.22, s32[]{:T(128)} %bitcast.23, s32[]{:T(128)} %bitcast.24, s32[]{:T(128)} %bitcast.26, s32[]{:T(128)} %bitcast.25, s32[]{:T(128)} %bitcast.10, ...), kind=kLoop, calls=%fused_computation.105 | loop fusion | flops 6144 | bytes 4140 | tf_op jit(solution)/shard_map/gather | solution.py:72
  24.6 5.7 %select_select_fusion.2 = s32[256]{0:T(256)S(1)} fusion(pred[256]{0:T(512)(128)(4,1)S(1)} %get-tuple-element.22, pred[256]{0:T(512)(128)(4,1)S(1)} %get-tuple-element.21, pred[256]{0:T(512)(128)(4,1)S(1)} %get-tuple-element.20, pred[256]{0:T(512)(128)(4,1)S(1)} %get-tuple-element.19, pred[256]{0:T(512)(128)(4,1)S(1)} %get-tuple-element.18, ...), kind=kLoop, calls=%fused_computation.137 | loop fusion | flops 2304 | bytes 4388 | tf_op jit(solution)/shard_map/gather | solution.py:72
  30.3 0.7 fusion.64
  31.0 8.8 %fusion.49 = (s32[256,1]{0,1:T(1,128)S(1)}, s32[256,1]{0,1:T(1,128)S(1)}) fusion(s32[]{:T(128)} %bitcast.71, s32[]{:T(128)} %bitcast.72, s32[]{:T(128)} %bitcast.73, s32[]{:T(128)} %bitcast.67, s32[]{:T(128)} %bitcast.74, s32[]{:T(128)} %bitcast.68, s32[]{:T(128)} %bitcast.76, s32[]{:T(128)} %bitcast.75, s32[]{:T(128)} %bitcast.70, s32[]{:T(128)} %bitcast.69, ...), kind=kLoop, calls=%fused_computation.132 | loop fusion | flops 11008 | bytes 3128 | tf_op jit(solution)/shard_map/mul | solution.py:112
  40.0 12.0 %all_gather.14 = bf16[16,576,16]{1,2,0:T(8,128)(2,1)S(1)} all-gather(bf16[2,576,16]{1,2,0:T(8,128)(2,1)} %param.34), channel_id=1, replica_groups=mesh['req'=8,'tp'=4] {'req'}, dimensions={0}, use_global_device_ids=true | all-gather | bytes 331776 | tf_op jit(solution)/shard_map/all_gather | solution.py:76
  52.0 12.0 %all_gather.13 = bf16[16,16,3,576]{3,1,2,0:T(8,128)(2,1)} all-gather(bf16[2,16,3,576]{3,1,2,0:T(8,128)(2,1)S(1)} %copy-done.14), channel_id=1, replica_groups=mesh['req'=8,'tp'=4] {'req'}, dimensions={0}, use_global_device_ids=true | all-gather | bytes 995328 | tf_op jit(solution)/shard_map/all_gather | solution.py:75
  64.2 6.8 %fusion.1 = f32[256,3,576]{0,2,1:T(8,128)} fusion(bf16[2304,3,576]{0,2,1:T(8,128)(2,1)} %param.26, bf16[256,2304]{1,0:T(8,128)(2,1)S(1)} %copy-done.5, f32[2304]{0:T(1024)S(1)} %copy-done.18, f32[256]{0:T(256)S(1)} %add_rsqrt_fusion.1), kind=kOutput, calls=%fused_computation.2 | convolution fusion | flops 2040791040 | bytes 10921984 | tf_op jit(solution)/shard_map/dot_general | solution.py:99
  71.0 1.5 copy-done.6
  72.5 1.1 slice-done
  73.6 1.2 fusion.25
  75.9 1.2 copy-done.8
  77.2 0.8 subtract_convert_fusion
  78.1 3.4 fusion.67
  81.5 2.2 convolution_convert_fusion.3
  84.1 2.5 fusion.8
  86.5 2.6 convolution_add_fusion
  90.3 1.1 reduce-window.28
  92.5 0.7 all_to_all.20
  93.1 3.4 all-to-all-start.1
  96.6 88.4 %all-reduce.3.cloned.1.call-done = f32[256,2304]{1,0:T(8,128)} async-done(((f32[256,2304]{1,0:T(8,128)}), f32[256,2304]{1,0:T(8,128)}) %all-reduce.3.cloned.1.call-update) | async-done | bytes 2359312 | tf_op jit(solution)/shard_map/psum | solution.py:154
  185.0 2.5 multiply_reduce_fusion
  188.5 1.0 copy-done.3
  190.9 3.7 %all-to-all-start.2 = ((bf16[8,72,16]{1,2,0:T(8,128)(2,1)}), bf16[8,72,16]{1,2,0:T(8,128)(2,1)S(1)}, u32[]{:S(2)}, u32[]{:S(2)}) async-start(bf16[8,72,16]{1,2,0:T(8,128)(2,1)} %copy.92), calls=%async_computation.2 | async-start | bytes 65536 | tf_op jit(solution)/shard_map/all_to_all | solution.py:200
  194.6 3.7 %convolution_convert_fusion = bf16[576,2304]{1,0:T(8,128)(2,1)} fusion(pred[256,576]{0,1:T(8,128)(4,1)S(1)} %fusion.17, bf16[256,2304]{1,0:T(8,128)(2,1)} %copy-done.3), kind=kOutput, calls=%fused_computation.8 | convolution fusion | flops 680804352 | bytes 3981312 | tf_op jit(solution)/shard_map/ts,td->sd/dot_general | solution.py:194
  198.2 1.2 all-to-all-done.2
  199.4 3.6 all-to-all-start
  203.5 32.1 %all-to-all-done = bf16[8,72,2304]{2,1,0:T(8,128)(2,1)S(1)} async-done(((bf16[8,72,2304]{2,1,0:T(8,128)(2,1)}), bf16[8,72,2304]{2,1,0:T(8,128)(2,1)S(1)}, u32[]{:S(2)}, u32[]{:S(2)}) %all-to-all-start) | async-done | bytes 2654240 | tf_op jit(solution)/shard_map/all_to_all | solution.py:197
  235.6 11.4 %fusion.72 = f32[576,2880]{1,0:T(8,128)S(1)} fusion(bf16[576,2304]{1,0:T(8,128)(2,1)S(1)} %bitcast.153, bf16[2304,2880]{0,1:T(8,128)(2,1)} %bitcast.173), kind=kOutput, calls=%fused_computation.165 | convolution fusion | flops 7644119040 | bytes 22560768 | tf_op jit(solution)/shard_map/dot_general | solution.py:216
  247.0 1.3 multiply_add_fusion
  248.3 9.2 %fusion.5 = bf16[576,2304]{1,0:T(8,128)(2,1)} fusion(bf16[1,1440,2304]{2,1,0:T(8,128)(2,1)} %param.30, f32[576,2880]{1,0:T(8,128)S(1)} %multiply_add_fusion), kind=kOutput, calls=%fused_computation.7 | convolution fusion | flops 3828363264 | bytes 16367616 | tf_op jit(solution)/shard_map/dot_general | solution.py:227
  257.5 4.5 %all-to-all-start.3 = ((bf16[8,72,2304]{2,1,0:T(8,128)(2,1)}), bf16[8,72,2304]{2,1,0:T(8,128)(2,1)}, u32[]{:S(2)}, u32[]{:S(2)}) async-start(bf16[8,72,2304]{2,1,0:T(8,128)(2,1)} %bitcast.152), calls=%async_computation.3 | async-start | bytes 5308416 | tf_op jit(solution)/shard_map/all_to_all | solution.py:230
  263.0 3.6 gather_fusion
  267.1 27.5 %all-to-all-done.3 = bf16[8,72,2304]{2,1,0:T(8,128)(2,1)} async-done(((bf16[8,72,2304]{2,1,0:T(8,128)(2,1)}), bf16[8,72,2304]{2,1,0:T(8,128)(2,1)}, u32[]{:S(2)}, u32[]{:S(2)}) %all-to-all-start.3) | async-done | bytes 2654240 | tf_op jit(solution)/shard_map/all_to_all | solution.py:230
  294.6 5.9 %convolution_convert_fusion.1 = bf16[256,2304]{1,0:T(8,128)(2,1)} fusion(f32[256,576]{0,1:T(8,128)S(1)} %select_reduce_fusion, bf16[576,2304]{1,0:T(8,128)(2,1)} %bitcast.65), kind=kOutput, calls=%fused_computation.12 | convolution fusion | flops 4077453312 | bytes 4423680 | tf_op jit(solution)/shard_map/dot_general | solution.py:236
  300.5 1.1 slice.135
  301.7 0.7 convolution_convert_fusion.2
  302.5 3.0 reshape.581
  305.5 6.7 %copy.94 = bf16[6,128,2,576]{1,3,2,0:T(8,128)(2,1)} copy(bf16[6,128,2,576]{3,2,1,0:T(2,128)(2,1)} %reshape.581) | data formatting | bytes 3538944
  312.2 41.7 %all-reduce.5.cloned.1.call-done = bf16[256,2304]{1,0:T(8,128)(2,1)} async-done(((bf16[256,2304]{1,0:T(8,128)(2,1)}), bf16[256,2304]{1,0:T(8,128)(2,1)}) %all-reduce.5.cloned.1.call-update) | async-done | bytes 1179664 | tf_op jit(solution)/shard_map/psum | solution.py:237
  353.8 3.7 %add_convert_fusion = bf16[256,2304]{1,0:T(8,128)(2,1)} fusion(bf16[256,2304]{1,0:T(8,128)(2,1)} %all-reduce.5.cloned.1.call-done, f32[256,2304]{1,0:T(8,128)} %all-reduce.3.cloned.1.call-done, bf16[256,2304]{1,0:T(8,128)(2,1)} %param.18), kind=kLoop, calls=%fused_computation.22 | loop fusion | flops 2949120 | bytes 5898240 | tf_op jit(solution)/shard_map/convert_element_type | solution.py:238
  (102 shorter events, 9.5 us)
Async XLA Ops:
  7.2 79.4 %copy-start = (bf16[576,2304]{1,0:T(8,128)(2,1)S(1)}, bf16[576,2304]{1,0:T(8,128)(2,1)}, u32[]{:S(2)}) copy-start(bf16[576,2304]{1,0:T(8,128)(2,1)} %param.27) | copy-start | bytes 7962628
  7.2 44.8 %copy-start.14 = (bf16[2,16,3,576]{3,1,2,0:T(8,128)(2,1)S(1)}, bf16[2,16,3,576]{3,1,2,0:T(8,128)(2,1)}, u32[]{:S(2)}) copy-start(bf16[2,16,3,576]{3,1,2,0:T(8,128)(2,1)} %param.33) | copy-start | bytes 331780
  7.2 57.0 %copy-start.18 = (f32[2304]{0:T(1024)S(1)}, f32[2304]{0:T(1024)}, u32[]{:S(2)}) copy-start(f32[2304]{0:T(1024)} %param.24) | copy-start | bytes 27652
  7.2 63.8 %all-gather.3.cloned.1.call-start = ((), (), s32[]{:S(2)}) async-start(), calls=%async_computation.4 | async-start | bytes 5308416 | tf_op jit(solution)/shard_map/all_gather | solution.py:74
  7.9 76.1 %all-gather.5.cloned.1.call-start = ((), (), s32[]{:S(2)}) async-start(), calls=%async_computation.5 | async-start | bytes 1327104 | tf_op jit(solution)/shard_map/all_gather | solution.py:77
  8.7 176.3 %all-reduce.3.cloned.1.call-start = ((), (), s32[]{:S(2)}) async-start(), calls=%async_computation.6 | async-start | bytes 4718592 | tf_op jit(solution)/shard_map/psum | solution.py:154
  10.4 53.8 %copy-start.5 = (bf16[256,2304]{1,0:T(8,128)(2,1)S(1)}, bf16[256,2304]{1,0:T(8,128)(2,1)}, u32[]{:S(2)}) copy-start(bf16[256,2304]{1,0:T(8,128)(2,1)} %param.18) | copy-start | bytes 3538948
  71.0 1.5 copy-start.6
  71.0 2.5 slice-start
  73.6 1.3 copy-start.9
  73.6 1.8 copy-start.10
  75.9 1.2 copy-start.8
  78.1 3.4 copy-start.12
  89.2 0.7 copy-start.16
  93.1 97.8 %all-to-all-start.1 = ((bf16[8,1,72]{2,1,0:T(2,128)(2,1)}), bf16[8,1,72]{2,1,0:T(2,128)(2,1)S(1)}, u32[]{:S(2)}, u32[]{:S(2)}) async-start(bf16[8,1,72]{2,1,0:T(2,128)(2,1)} %all_to_all.20), calls=%async_computation.1 | async-start | bytes 8192 | tf_op jit(solution)/shard_map/all_to_all | solution.py:203
  96.6 90.9 %copy-start.17 = (f32[2304]{0:T(1024)S(1)}, f32[2304]{0:T(1024)}, u32[]{:S(2)}) copy-start(f32[2304]{0:T(1024)} %param.25) | copy-start | bytes 27652
  185.0 2.7 copy-start.2
  185.0 3.0 copy-start.7
  188.0 1.5 slice-start.1
  188.4 1.0 copy-start.3
  190.9 8.5 %all-to-all-start.2 = ((bf16[8,72,16]{1,2,0:T(8,128)(2,1)}), bf16[8,72,16]{1,2,0:T(8,128)(2,1)S(1)}, u32[]{:S(2)}, u32[]{:S(2)}) async-start(bf16[8,72,16]{1,2,0:T(8,128)(2,1)} %copy.92), calls=%async_computation.2 | async-start | bytes 65536 | tf_op jit(solution)/shard_map/all_to_all | solution.py:200
  199.4 36.2 %all-to-all-start = ((bf16[8,72,2304]{2,1,0:T(8,128)(2,1)}), bf16[8,72,2304]{2,1,0:T(8,128)(2,1)S(1)}, u32[]{:S(2)}, u32[]{:S(2)}) async-start(bf16[8,72,2304]{2,1,0:T(8,128)(2,1)} %bitcast.55), calls=%async_computation | async-start | bytes 5308416 | tf_op jit(solution)/shard_map/all_to_all | solution.py:197
  235.6 11.4 %copy-start.11 = (bf16[1,256,2,1440]{1,3,2,0:T(8,128)(2,1)S(1)}, bf16[1,256,2,1440]{1,3,2,0:T(8,128)(2,1)}, u32[]{:S(2)}) copy-start(bf16[1,256,2,1440]{1,3,2,0:T(8,128)(2,1)} %param.31) | copy-start | bytes 4423684
  257.5 5.1 %copy-start.4 = (bf16[256,2304]{1,0:T(8,128)(2,1)S(1)}, bf16[256,2304]{1,0:T(8,128)(2,1)}, u32[]{:S(2)}) copy-start(bf16[256,2304]{1,0:T(8,128)(2,1)} %copy-done.3) | copy-start | bytes 3538948
  257.5 5.1 %copy-start.15 = (bf16[2304,8]{0,1:T(8,128)(2,1)S(1)}, bf16[2304,8]{0,1:T(8,128)(2,1)}, u32[]{:S(2)}) copy-start(bf16[2304,8]{0,1:T(8,128)(2,1)} %param.28) | copy-start | bytes 110596
  257.5 37.1 %all-to-all-start.3 = ((bf16[8,72,2304]{2,1,0:T(8,128)(2,1)}), bf16[8,72,2304]{2,1,0:T(8,128)(2,1)}, u32[]{:S(2)}, u32[]{:S(2)}) async-start(bf16[8,72,2304]{2,1,0:T(8,128)(2,1)} %bitcast.152), calls=%async_computation.3 | async-start | bytes 5308416 | tf_op jit(solution)/shard_map/all_to_all | solution.py:230
  262.0 91.8 %all-reduce.5.cloned.1.call-start = ((), (), s32[]{:S(2)}) async-start(), calls=%async_computation.7 | async-start | bytes 2359296 | tf_op jit(solution)/shard_map/psum | solution.py:237
  294.6 7.0 %copy-start.13 = (bf16[256,9,32]{0,2,1:T(8,128)(2,1)S(1)}, bf16[256,9,32]{0,2,1:T(8,128)(2,1)}, u32[]{:S(2)}) copy-start(bf16[256,9,32]{0,2,1:T(8,128)(2,1)} %copy-done.12) | copy-start | bytes 442372
  305.5 52.0 %copy-start.1 = (bf16[576,2304]{1,0:T(8,128)(2,1)S(1)}, bf16[576,2304]{1,0:T(8,128)(2,1)}, u32[]{:S(2)}) copy-start(bf16[576,2304]{1,0:T(8,128)(2,1)} %param.27) | copy-start | bytes 7962628
Sparse Core Ops, SparseCore 0:
  9.9 42.8 all-gather.2
  54.7 24.0 all-gather.4
  89.3 95.5 all-reduce.2
  300.6 53.1 all-reduce.4
where the time goes:
time: 365 us; the launch traced here: 364 us
  waiting for transfers between devices  192 us (53%)
  matrix products  52.9 us (14%)
  other arithmetic  35.5 us (10%)
  local copies, waits for them, and re-layouts  29.5 us (8%)
  blocking collectives  24 us (7%)
  starting transfers between devices  15.6 us (4%)
  between operations  14.2 us (4%)
    psum x1, waiting for transfers between devices, per_device(): mixed_out = lax.psum(head_term, 'tp')  88.4 us
    psum x1, waiting for transfers between devices, per_device(): moe_sum = lax.psum(moe_part.astype(jnp.bfloat16), 'tp').astype(jnp.float32)  41.7 us
    all_to_all x1, waiting for transfers between devices, per_device(): lax.all_to_all(spread_copies(send_rows), 'req', split_axis=0, concat_axis...  32.1 us
    all_to_all x1, waiting for transfers between devices, per_device(): lax.all_to_all(partial_term.reshape(n_req, count, D), 'req', split_axis=0...  27.5 us
    gather x3, other arithmetic, per_device(): token_slot = slot_of[adapter]  12.5 us
    unnamed x40, local copies, waits for them, and re-layouts  12.2 us
    all_gather x1, blocking collectives, per_device(): lax.all_gather(pool_aout, 'req', axis=0, tiled=True)  12 us
    all_gather x1, blocking collectives, per_device(): lax.all_gather(slot_query_key_value_up, 'req', axis=0, tiled=True)  12 us
  transfers between devices with their start and end apart: 8, of which 5 were waited for; matrix products, arithmetic and copies ran while one was open for 20% of the time, Pallas kernels for 0%

commit v1 on v0

--- a/solution.py
+++ b/solution.py
@@ -151,7 +151,11 @@
         jnp.dot(attention_result, output_weight, preferred_element_type=jnp.float32)
         + adapter_scale * output_update
     )
-    mixed_out = lax.psum(head_term, "tp")
+    mixed_out = head_term
+    for hop in (1, 2):
+        mixed_out = mixed_out + lax.ppermute(
+            mixed_out, "tp", [(dev, dev ^ hop) for dev in range(4)]
+        )
     residual_stream = activations.astype(jnp.float32) + mixed_out
     normed_moe = rms_norm(residual_stream, moe_gain).astype(jnp.bfloat16)
     logits = jnp.dot(normed_moe, router, preferred_element_type=jnp.float32)

time: 365 us -> 428 us (1.17)
  waiting for transfers between devices: 192 us -> 253 us
    ppermute x0 -> x2, waiting for transfers between devices: none -> 147 us  [per_device(): lax.ppermute(mixed_out, 'tp', [(dev, dev ^ hop) for dev in range(4)])]
    psum x1 -> x0, waiting for transfers between devices: 88.4 us -> none  [per_device(): mixed_out = lax.psum(head_term, 'tp')]
  transfers between devices with their start and end apart: 8 -> 9, of which waited for: 5 -> 6; matrix products, arithmetic and copies ran while one was open for 20% -> 18% of each run, Pallas kernels for 0% -> 0%
where the time goes in v1:
time: 428 us; the launch traced here: 427 us
  waiting for transfers between devices  253 us (59%)
  matrix products  51.4 us (12%)
  other arithmetic  35.7 us (8%)
  local copies, waits for them, and re-layouts  29.2 us (7%)
  blocking collectives  24 us (6%)
  starting transfers between devices  19.4 us (5%)
  between operations  14.3 us (3%)
    ppermute x2, waiting for transfers between devices, per_device(): lax.ppermute(mixed_out, 'tp', [(dev, dev ^ hop) for dev in range(4)])  147 us
    psum x1, waiting for transfers between devices, per_device(): moe_sum = lax.psum(moe_part.astype(jnp.bfloat16), 'tp').astype(jnp.float32)  43.6 us
    all_to_all x1, waiting for transfers between devices, per_device(): lax.all_to_all(spread_copies(send_rows), 'req', split_axis=0, concat_axis...  32.1 us
    all_to_all x1, waiting for transfers between devices, per_device(): lax.all_to_all(partial_term.reshape(n_req, count, D), 'req', split_axis=0...  27.5 us
    gather x3, other arithmetic, per_device(): token_slot = slot_of[adapter]  12.5 us
    all_gather x1, blocking collectives, per_device(): lax.all_gather(pool_aout, 'req', axis=0, tiled=True)  12 us
    all_gather x1, blocking collectives, per_device(): lax.all_gather(slot_query_key_value_up, 'req', axis=0, tiled=True)  12 us
    dot_general x1, matrix products, per_device(): jnp.dot(flat_rows, w_gate_up[0].reshape(D, 2 * unit_count), preferred_ele...  11.4 us
  transfers between devices with their start and end apart: 9, of which 6 were waited for; matrix products, arithmetic and copies ran while one was open for 18% of the time, Pallas kernels for 0%

profile of v1, /device:TPU:0, one launch (start us, length us, event | category | flops | bytes accessed | tf_op | source)
XLA Modules:
  0.0 426.7 jit_solution(7913849905272580634)
XLA Ops:
  8.0 0.7 all-gather.5.cloned.1.call-update
  9.4 0.8 reduce-window.27
  10.4 0.8 bitcast_subtract_fusion.2
  11.2 1.6 fusion.10
  12.8 1.5 fusion.63
  14.3 1.5 fusion.66
  15.8 2.0 fusion.62
  17.8 6.8 %compare_select_fusion.9 = (s32[256,1]{0,1:T(1,128)S(1)}, s32[256,1]{0,1:T(1,128)S(1)}, s32[256,1]{0,1:T(1,128)S(1)}) fusion(s32[]{:T(128)} %bitcast.20, s32[]{:T(128)} %bitcast.21, s32[]{:T(128)} %bitcast.22, s32[]{:T(128)} %bitcast.23, s32[]{:T(128)} %bitcast.24, s32[]{:T(128)} %bitcast.26, s32[]{:T(128)} %bitcast.25, s32[]{:T(128)} %bitcast.10, ...), kind=kLoop, calls=%fused_computation.105 | loop fusion | flops 6144 | bytes 4140 | tf_op jit(solution)/shard_map/gather | solution.py:72
  24.6 5.7 %select_select_fusion.2 = s32[256]{0:T(256)S(1)} fusion(pred[256]{0:T(512)(128)(4,1)S(1)} %get-tuple-element.22, pred[256]{0:T(512)(128)(4,1)S(1)} %get-tuple-element.21, pred[256]{0:T(512)(128)(4,1)S(1)} %get-tuple-element.20, pred[256]{0:T(512)(128)(4,1)S(1)} %get-tuple-element.19, pred[256]{0:T(512)(128)(4,1)S(1)} %get-tuple-element.18, ...), kind=kLoop, calls=%fused_computation.137 | loop fusion | flops 2304 | bytes 4388 | tf_op jit(solution)/shard_map/gather | solution.py:72
  31.0 8.8 %fusion.49 = (s32[256,1]{0,1:T(1,128)S(1)}, s32[256,1]{0,1:T(1,128)S(1)}) fusion(s32[]{:T(128)} %bitcast.71, s32[]{:T(128)} %bitcast.72, s32[]{:T(128)} %bitcast.73, s32[]{:T(128)} %bitcast.67, s32[]{:T(128)} %bitcast.74, s32[]{:T(128)} %bitcast.68, s32[]{:T(128)} %bitcast.76, s32[]{:T(128)} %bitcast.75, s32[]{:T(128)} %bitcast.70, s32[]{:T(128)} %bitcast.69, ...), kind=kLoop, calls=%fused_computation.132 | loop fusion | flops 11008 | bytes 3128 | tf_op jit(solution)/shard_map/mul | solution.py:112
  40.0 12.0 %all_gather.14 = bf16[16,576,16]{1,2,0:T(8,128)(2,1)S(1)} all-gather(bf16[2,576,16]{1,2,0:T(8,128)(2,1)} %param.34), channel_id=1, replica_groups=mesh['req'=8,'tp'=4] {'req'}, dimensions={0}, use_global_device_ids=true | all-gather | bytes 331776 | tf_op jit(solution)/shard_map/all_gather | solution.py:76
  52.0 12.0 %all_gather.13 = bf16[16,16,3,576]{3,1,2,0:T(8,128)(2,1)} all-gather(bf16[2,16,3,576]{3,1,2,0:T(8,128)(2,1)S(1)} %copy-done.14), channel_id=1, replica_groups=mesh['req'=8,'tp'=4] {'req'}, dimensions={0}, use_global_device_ids=true | all-gather | bytes 995328 | tf_op jit(solution)/shard_map/all_gather | solution.py:75
  64.2 6.8 %fusion.1 = f32[256,3,576]{0,2,1:T(8,128)} fusion(bf16[2304,3,576]{0,2,1:T(8,128)(2,1)} %param.26, bf16[256,2304]{1,0:T(8,128)(2,1)S(1)} %copy-done.7, f32[2304]{0:T(1024)S(1)} %copy-done.18, f32[256]{0:T(256)S(1)} %add_rsqrt_fusion.1), kind=kOutput, calls=%fused_computation.2 | convolution fusion | flops 2040791040 | bytes 10921984 | tf_op jit(solution)/shard_map/dot_general | solution.py:99
  71.0 1.5 copy-done.8
  72.4 1.1 slice-done
  73.5 1.2 fusion.25
  75.8 1.2 copy-done.6
  77.1 0.8 subtract_convert_fusion
  78.0 3.4 fusion.67
  81.5 2.2 convolution_convert_fusion.3
  84.0 2.5 fusion.8
  86.5 1.1 convolution_add_fusion
  87.7 1.6 collective-permute-start
  89.3 52.0 %collective-permute-done = f32[256,2304]{1,0:T(8,128)S(1)} collective-permute-done((f32[256,2304]{1,0:T(8,128)S(1)}, f32[256,2304]{1,0:T(8,128)S(1)}, u32[]{:S(2)}, u32[]{:S(2)}) %collective-permute-start) | collective-permute-done | bytes 2359328 | tf_op jit(solution)/shard_map/ppermute | solution.py:156
  141.5 2.5 collective-permute-start.1
  144.5 1.1 reduce-window.28
  147.3 3.5 all-to-all-start.1
  150.8 95.0 %collective-permute-done.1 = f32[256,2304]{1,0:T(8,128)} collective-permute-done((f32[256,2304]{1,0:T(8,128)S(1)}, f32[256,2304]{1,0:T(8,128)}, u32[]{:S(2)}, u32[]{:S(2)}) %collective-permute-start.1) | collective-permute-done | bytes 2359328 | tf_op jit(solution)/shard_map/ppermute | solution.py:156
  245.9 3.2 multiply_reduce_fusion
  249.3 1.8 slice-done.1
  252.6 3.3 all-to-all-start.2
  256.0 3.7 convolution_convert_fusion
  259.6 1.1 all-to-all-done.2
  260.7 3.6 all-to-all-start
  264.8 32.1 %all-to-all-done = bf16[8,72,2304]{2,1,0:T(8,128)(2,1)S(1)} async-done(((bf16[8,72,2304]{2,1,0:T(8,128)(2,1)}), bf16[8,72,2304]{2,1,0:T(8,128)(2,1)S(1)}, u32[]{:S(2)}, u32[]{:S(2)}) %all-to-all-start) | async-done | bytes 2654240 | tf_op jit(solution)/shard_map/all_to_all | solution.py:201
  296.9 11.4 %fusion.72 = f32[576,2880]{1,0:T(8,128)S(1)} fusion(bf16[576,2304]{1,0:T(8,128)(2,1)S(1)} %bitcast.153, bf16[2304,2880]{0,1:T(8,128)(2,1)} %bitcast.173), kind=kOutput, calls=%fused_computation.165 | convolution fusion | flops 7644119040 | bytes 22560768 | tf_op jit(solution)/shard_map/dot_general | solution.py:220
  308.3 1.3 multiply_add_fusion
  309.6 9.2 %fusion.5 = bf16[576,2304]{1,0:T(8,128)(2,1)} fusion(bf16[1,1440,2304]{2,1,0:T(8,128)(2,1)} %param.30, f32[576,2880]{1,0:T(8,128)S(1)} %multiply_add_fusion), kind=kOutput, calls=%fused_computation.7 | convolution fusion | flops 3828363264 | bytes 16367616 | tf_op jit(solution)/shard_map/dot_general | solution.py:231
  318.8 4.5 %all-to-all-start.3 = ((bf16[8,72,2304]{2,1,0:T(8,128)(2,1)}), bf16[8,72,2304]{2,1,0:T(8,128)(2,1)}, u32[]{:S(2)}, u32[]{:S(2)}) async-start(bf16[8,72,2304]{2,1,0:T(8,128)(2,1)} %bitcast.152), calls=%async_computation.3 | async-start | bytes 5308416 | tf_op jit(solution)/shard_map/all_to_all | solution.py:234
  324.3 3.6 gather_fusion
  328.4 27.5 %all-to-all-done.3 = bf16[8,72,2304]{2,1,0:T(8,128)(2,1)} async-done(((bf16[8,72,2304]{2,1,0:T(8,128)(2,1)}), bf16[8,72,2304]{2,1,0:T(8,128)(2,1)}, u32[]{:S(2)}, u32[]{:S(2)}) %all-to-all-start.3) | async-done | bytes 2654240 | tf_op jit(solution)/shard_map/all_to_all | solution.py:234
  355.9 5.9 %convolution_convert_fusion.1 = bf16[256,2304]{1,0:T(8,128)(2,1)} fusion(f32[256,576]{0,1:T(8,128)S(1)} %select_reduce_fusion, bf16[576,2304]{1,0:T(8,128)(2,1)} %bitcast.65), kind=kOutput, calls=%fused_computation.12 | convolution fusion | flops 4077453312 | bytes 4423680 | tf_op jit(solution)/shard_map/dot_general | solution.py:240
  361.8 1.1 slice.135
  363.0 0.7 convolution_convert_fusion.2
  363.8 3.0 reshape.581
  366.8 6.7 %copy.94 = bf16[6,128,2,576]{1,3,2,0:T(8,128)(2,1)} copy(bf16[6,128,2,576]{3,2,1,0:T(2,128)(2,1)} %reshape.581) | data formatting | bytes 3538944
  373.4 43.6 %all-reduce.2.cloned.1.call-done = bf16[256,2304]{1,0:T(8,128)(2,1)} async-done(((bf16[256,2304]{1,0:T(8,128)(2,1)}), bf16[256,2304]{1,0:T(8,128)(2,1)}) %all-reduce.2.cloned.1.call-update) | async-done | bytes 1179664 | tf_op jit(solution)/shard_map/psum | solution.py:241
  417.0 3.2 add_convert_fusion
  (104 shorter events, 10.4 us)
Async XLA Ops:
  7.2 79.3 %copy-start = (bf16[576,2304]{1,0:T(8,128)(2,1)S(1)}, bf16[576,2304]{1,0:T(8,128)(2,1)}, u32[]{:S(2)}) copy-start(bf16[576,2304]{1,0:T(8,128)(2,1)} %param.27) | copy-start | bytes 7962628
  7.2 44.8 %copy-start.14 = (bf16[2,16,3,576]{3,1,2,0:T(8,128)(2,1)S(1)}, bf16[2,16,3,576]{3,1,2,0:T(8,128)(2,1)}, u32[]{:S(2)}) copy-start(bf16[2,16,3,576]{3,1,2,0:T(8,128)(2,1)} %param.33) | copy-start | bytes 331780
  7.2 56.9 %copy-start.18 = (f32[2304]{0:T(1024)S(1)}, f32[2304]{0:T(1024)}, u32[]{:S(2)}) copy-start(f32[2304]{0:T(1024)} %param.24) | copy-start | bytes 27652
  7.2 63.8 %all-gather.3.cloned.1.call-start = ((), (), s32[]{:S(2)}) async-start(), calls=%async_computation.4 | async-start | bytes 5308416 | tf_op jit(solution)/shard_map/all_gather | solution.py:74
  7.9 76.1 %all-gather.5.cloned.1.call-start = ((), (), s32[]{:S(2)}) async-start(), calls=%async_computation.5 | async-start | bytes 1327104 | tf_op jit(solution)/shard_map/all_gather | solution.py:77
  10.4 53.8 %copy-start.7 = (bf16[256,2304]{1,0:T(8,128)(2,1)S(1)}, bf16[256,2304]{1,0:T(8,128)(2,1)}, u32[]{:S(2)}) copy-start(bf16[256,2304]{1,0:T(8,128)(2,1)} %param.18) | copy-start | bytes 3538948
  71.0 1.5 copy-start.8
  71.0 2.5 slice-start
  73.5 1.3 copy-start.9
  73.5 1.8 copy-start.10
  75.8 1.2 copy-start.6
  78.0 3.4 copy-start.12
  87.7 56.3 %copy-start.16 = (s32[256,2]{0,1:T(2,128)S(1)}, s32[256,2]{0,1:T(2,128)}, u32[]{:S(2)}) copy-start(s32[256,2]{0,1:T(2,128)} %param.23) | copy-start | bytes 6148
  87.7 53.6 %collective-permute-start = (f32[256,2304]{1,0:T(8,128)S(1)}, f32[256,2304]{1,0:T(8,128)S(1)}, u32[]{:S(2)}, u32[]{:S(2)}) collective-permute-start(f32[256,2304]{1,0:T(8,128)S(1)} %convolution_add_fusion), channel_id=1, source_target_pairs={{0,1},{1,0},{2,3},{3,2},{4,5},{5,4},{6,7},{7,6},{8,9},{9,8},{10,11... | collective-permute-start | bytes 7077896 | tf_op jit(solution)/shard_map/ppermute | solution.py:156
  141.5 9.3 %copy-start.5 = (f32[256,2304]{1,0:T(8,128)}, f32[256,2304]{1,0:T(8,128)S(1)}, u32[]{:S(2)}) copy-start(f32[256,2304]{1,0:T(8,128)S(1)} %add.170) | copy-start | bytes 7077892
  141.5 104.3 %collective-permute-start.1 = (f32[256,2304]{1,0:T(8,128)S(1)}, f32[256,2304]{1,0:T(8,128)}, u32[]{:S(2)}, u32[]{:S(2)}) collective-permute-start(f32[256,2304]{1,0:T(8,128)S(1)} %add.170), channel_id=1, source_target_pairs={{0,2},{1,3},{2,0},{3,1},{4,6},{5,7},{6,4},{7,5},{8,10},{9,11},{10,... | collective-permute-start | bytes 7077896 | tf_op jit(solution)/shard_map/ppermute | solution.py:156
  147.3 105.3 %all-to-all-start.1 = ((bf16[8,1,72]{2,1,0:T(2,128)(2,1)}), bf16[8,1,72]{2,1,0:T(2,128)(2,1)S(1)}, u32[]{:S(2)}, u32[]{:S(2)}) async-start(bf16[8,1,72]{2,1,0:T(2,128)(2,1)} %all_to_all.20), calls=%async_computation.1 | async-start | bytes 8192 | tf_op jit(solution)/shard_map/all_to_all | solution.py:207
  150.8 98.2 %copy-start.17 = (f32[2304]{0:T(1024)S(1)}, f32[2304]{0:T(1024)}, u32[]{:S(2)}) copy-start(f32[2304]{0:T(1024)} %param.25) | copy-start | bytes 27652
  249.0 2.6 copy-start.2
  249.0 2.1 slice-start.1
  249.3 2.3 copy-start.3
  252.6 8.1 %all-to-all-start.2 = ((bf16[8,72,16]{1,2,0:T(8,128)(2,1)}), bf16[8,72,16]{1,2,0:T(8,128)(2,1)S(1)}, u32[]{:S(2)}, u32[]{:S(2)}) async-start(bf16[8,72,16]{1,2,0:T(8,128)(2,1)} %copy.92), calls=%async_computation.2 | async-start | bytes 65536 | tf_op jit(solution)/shard_map/all_to_all | solution.py:204
  260.7 36.2 %all-to-all-start = ((bf16[8,72,2304]{2,1,0:T(8,128)(2,1)}), bf16[8,72,2304]{2,1,0:T(8,128)(2,1)S(1)}, u32[]{:S(2)}, u32[]{:S(2)}) async-start(bf16[8,72,2304]{2,1,0:T(8,128)(2,1)} %bitcast.55), calls=%async_computation | async-start | bytes 5308416 | tf_op jit(solution)/shard_map/all_to_all | solution.py:201
  296.9 11.4 %copy-start.11 = (bf16[1,256,2,1440]{1,3,2,0:T(8,128)(2,1)S(1)}, bf16[1,256,2,1440]{1,3,2,0:T(8,128)(2,1)}, u32[]{:S(2)}) copy-start(bf16[1,256,2,1440]{1,3,2,0:T(8,128)(2,1)} %param.31) | copy-start | bytes 4423684
  318.8 5.1 %copy-start.4 = (bf16[256,2304]{1,0:T(8,128)(2,1)S(1)}, bf16[256,2304]{1,0:T(8,128)(2,1)}, u32[]{:S(2)}) copy-start(bf16[256,2304]{1,0:T(8,128)(2,1)} %copy-done.3) | copy-start | bytes 3538948
  318.8 5.1 %copy-start.15 = (bf16[2304,8]{0,1:T(8,128)(2,1)S(1)}, bf16[2304,8]{0,1:T(8,128)(2,1)}, u32[]{:S(2)}) copy-start(bf16[2304,8]{0,1:T(8,128)(2,1)} %param.28) | copy-start | bytes 110596
  318.8 37.1 %all-to-all-start.3 = ((bf16[8,72,2304]{2,1,0:T(8,128)(2,1)}), bf16[8,72,2304]{2,1,0:T(8,128)(2,1)}, u32[]{:S(2)}, u32[]{:S(2)}) async-start(bf16[8,72,2304]{2,1,0:T(8,128)(2,1)} %bitcast.152), calls=%async_computation.3 | async-start | bytes 5308416 | tf_op jit(solution)/shard_map/all_to_all | solution.py:234
  323.3 93.7 %all-reduce.2.cloned.1.call-start = ((), (), s32[]{:S(2)}) async-start(), calls=%async_computation.6 | async-start | bytes 2359296 | tf_op jit(solution)/shard_map/psum | solution.py:241
  355.9 7.0 %copy-start.13 = (bf16[256,9,32]{0,2,1:T(8,128)(2,1)S(1)}, bf16[256,9,32]{0,2,1:T(8,128)(2,1)}, u32[]{:S(2)}) copy-start(bf16[256,9,32]{0,2,1:T(8,128)(2,1)} %copy-done.12) | copy-start | bytes 442372
  366.8 53.4 %copy-start.1 = (bf16[576,2304]{1,0:T(8,128)(2,1)S(1)}, bf16[576,2304]{1,0:T(8,128)(2,1)}, u32[]{:S(2)}) copy-start(bf16[576,2304]{1,0:T(8,128)(2,1)} %param.27) | copy-start | bytes 7962628
Sparse Core Ops, SparseCore 0:
  9.9 42.8 all-gather.2
  54.7 24.0 all-gather.4
  361.9 55.0 all-reduce.1
